TPU v7x, 32 devices: a whole 2x2x4 slice. The times are simulated.
32 devices in a mesh: row: 8 (over z, x), col: 4 (over y, core).
Axes of the slice: x: 2, y: 2, z: 4, core: 2. Of those that a mesh axis runs over, the one named last changes fastest.
Arguments:
- pole_values: float32 [16384], P('row'), may hold values from 0.3 to 127.9, as said below
- rank_one: float32 [16384], P('row'), may hold values from -6 to 6
- deflated: int32 [16384], P('row'), may hold values 0 or 1
- onsite_energy: float32 [16384], P('row'), may hold values from 0.5 to 3
- secular_roots: float32 [16, 256], replicated, may hold values from 0 to 127.7, as said below
- column_order: int32 [16, 256], replicated, may hold values from 0 to 255, each once within a row
- q_blocks: bfloat16 [32, 512, 512], P('row'), may hold values from -1 to 1, as said below
- diag_blocks: float32 [32, 512, 512], P('row'), may hold values from -0.15625 to 0.15625
- coupling_blocks: float32 [32, 512, 512], P('row'), may hold values from -0.15625 to 0.15625
Outputs:
- refined_panel: float32 [16, 16384, 256], P(None, 'row', 'col')
- new_roots: float32 [16, 256], P(None, 'col')
Inputs may be any that keep to these rules, and one draw needn't show every extreme that they name: `pole_values`: every pole lies 0.3 to 0.4 above a multiple of 0.5, at most 0.5 * 256 - 0.1. `secular_roots`: the root of index j in a panel lies between 0.5 j and 0.5 j + 0.2. `q_blocks`: each block is an orthogonal matrix rounded to bfloat16.
All inputs are finite; a program needn't handle non-finite values. No bound on the sum of `deflated` on one device may be relied on, other than what follows from the above.
Results may differ from a plain program's by a relative error of at most 0.0004.
The roundings to bfloat16 on the way count: a program that leaves them out, or rounds other values in their place, can miss the bound.
Values may be sent and summed in bfloat16 or wider, within the bound.
A program may use at most 192 MiB of HBM per device.

v0:
```python
import jax
import jax.numpy as jnp
from jax import lax
from jax.sharding import PartitionSpec as P

EPSILON = 1e-06
HIGHEST = lax.Precision.HIGHEST


def from_behind(value, axis, steps):
    count = lax.axis_size(axis)
    initial, last = (max(0, -steps), min(count, count - steps))
    return lax.ppermute(value, axis, [(source, source + steps) for source in range(initial, last)])


def with_halo(block, sides, width):
    for axis, dim in sides:
        count = lax.axis_size(axis)
        forward = [(i, i + 1) for i in range(count - 1)]
        backward = [(target, source) for source, target in forward]
        low = lax.ppermute(
            lax.slice_in_dim(block, block.shape[dim] - width, None, axis=dim), axis, forward
        )
        high = lax.ppermute(lax.slice_in_dim(block, 0, width, axis=dim), axis, backward)
        block = jnp.concatenate([low, block, high], axis=dim)
    return block


def pick_roots(secular_roots, column_order):
    panel_slots = jnp.arange(secular_roots.shape[1], dtype=jnp.int32)
    selector = (column_order[:, :, None] == panel_slots[None, None, :]).astype(jnp.float32)
    return jnp.sum(selector * secular_roots[:, None, :], axis=2)


def form_panel(chosen, pole_values, weights, q_blocks):
    cauchy = weights[None, :, None] / (pole_values[None, :, None] - chosen[:, None, :])
    column_squares = lax.psum(jnp.sum(cauchy * cauchy, axis=1), "row")
    factor = lax.rsqrt(column_squares + EPSILON)
    scaled = (cauchy * factor[:, None, :]).astype(jnp.bfloat16)
    panels, rows_here, columns = scaled.shape
    block_count = q_blocks.shape[0]
    block_size = q_blocks.shape[1]
    blocked = scaled.reshape(panels, block_count, block_size, columns)
    formed = jnp.einsum("bij,pbjc->pbic", q_blocks, blocked, preferred_element_type=jnp.float32)
    return (formed.astype(jnp.bfloat16).reshape(panels, rows_here, columns), factor)


def apply_operator(padded, onsite_energy, diag_blocks, coupling_blocks):
    panels = padded.shape[0]
    columns = padded.shape[2]
    block_count = diag_blocks.shape[0]
    block_size = diag_blocks.shape[1]
    following = from_behind(coupling_blocks[0].astype(jnp.bfloat16), "row", -1).astype(jnp.float32)
    blocked_rows = padded.astype(jnp.float32).reshape(panels, block_count + 2, block_size, columns)
    middle = blocked_rows[:, 1:-1]
    lower_rows = blocked_rows[:, :-2]
    upper_rows = blocked_rows[:, 2:]
    upper_blocks = jnp.concatenate([coupling_blocks[1:], following[None]], axis=0)
    symmetric = 0.5 * (diag_blocks + jnp.swapaxes(diag_blocks, 1, 2))
    operated = jnp.einsum("bij,pbjc->pbic", symmetric, middle, precision=HIGHEST)
    operated = operated + jnp.einsum(
        "bij,pbjc->pbic", coupling_blocks, lower_rows, precision=HIGHEST
    )
    operated = operated + jnp.einsum("bji,pbjc->pbic", upper_blocks, upper_rows, precision=HIGHEST)
    operated = operated + onsite_energy.reshape(block_count, block_size)[None, :, :, None] * middle
    return operated.reshape(panels, block_count * block_size, columns)


def build_update(residual, projected, roots_left, roots_right, on_diagonal):
    spacing = roots_right - roots_left + on_diagonal.astype(jnp.float32)
    return jnp.where(on_diagonal, 0.5 * residual, (projected + roots_right * residual) / spacing)


def shards(
    pole_values,
    rank_one,
    deflated,
    onsite_energy,
    secular_roots,
    column_order,
    q_blocks,
    diag_blocks,
    coupling_blocks,
):
    col_count = lax.axis_size("col")
    row_count = lax.axis_size("row")
    block_size = q_blocks.shape[1]
    weights = rank_one * (1 - deflated).astype(jnp.float32)
    chosen_all = pick_roots(secular_roots, column_order)
    panel_size = secular_roots.shape[1]
    columns = panel_size // col_count
    offset = lax.axis_index("col") * columns
    chosen = lax.dynamic_slice_in_dim(chosen_all, offset, columns, 1)
    own_cols, own_factor = form_panel(chosen, pole_values, weights, q_blocks)
    all_cols = lax.all_gather(own_cols, "col", axis=2, tiled=True)
    padded = with_halo(own_cols, (("row", 1),), block_size)
    operated = apply_operator(padded, onsite_energy, diag_blocks, coupling_blocks)
    all_float = all_cols.astype(jnp.float32)
    own_float = own_cols.astype(jnp.float32)
    column_numbers = offset + jnp.arange(columns, dtype=jnp.int32)
    gram = jnp.einsum("pri,prj->pij", all_cols, own_cols, preferred_element_type=jnp.float32)
    projected = jnp.einsum("pri,prj->pij", all_float, operated, precision=HIGHEST)
    gram, projected = lax.psum((gram, projected), "row")
    panel_slots = jnp.arange(panel_size, dtype=jnp.int32)
    on_diagonal = (panel_slots[:, None] == column_numbers[None, :])[None, :, :]
    residual = on_diagonal.astype(jnp.float32) - gram
    update = build_update(
        residual, projected, chosen_all[:, :, None], chosen[:, None, :], on_diagonal
    )
    diag_gram = jnp.sum(jnp.where(on_diagonal, gram, 0.0), axis=1)
    diag_proj = jnp.sum(jnp.where(on_diagonal, projected, 0.0), axis=1)
    updated = own_float + jnp.einsum("pri,pij->prj", all_float, update, precision=HIGHEST)
    column_sums = lax.psum(jnp.sum(updated * updated, axis=1), "row")
    matrix_order = float(own_cols.shape[1] * row_count)
    refined = updated * jnp.sqrt(matrix_order / column_sums)[:, None, :]
    return (refined, diag_proj / diag_gram)


def solution(mesh):
    placed = (
        P("row"),
        P("row"),
        P("row"),
        P("row"),
        P(),
        P(),
        P("row", None, None),
        P("row", None, None),
        P("row", None, None),
    )
    return jax.shard_map(
        shards,
        mesh=mesh,
        in_specs=placed,
        out_specs=(P(None, "row", "col"), P(None, "col")),
        check_vma=False,
    )
```

profile of v0, /device:TPU:0, one launch (start us, length us, event | category | flops | bytes accessed | tf_op | source)
XLA Modules:
  0.0 367.3 jit_solution(1254542976846287649)
XLA Ops:
  8.8 2.0 select_reduce_fusion
  10.9 2.4 multiply_reduce_fusion.1
  13.3 23.3 %psum.28 = f32[16,64]{1,0:T(8,128)S(1)} all-reduce(f32[16,64]{1,0:T(8,128)S(1)} %multiply_reduce_fusion.1), channel_id=1, replica_groups=mesh['row'=8,'col'=4] {'row'}, use_global_device_ids=true, to_apply=%region_2.0 | all-reduce | flops 1024 | bytes 8192 | tf_op jit(solution)/shard_map/psum | solution.py:37
  36.6 2.7 convert_bitcast_fusion
  39.3 2.7 copy.34
  42.1 3.1 fusion.43
  49.4 1.6 collective-permute-start.2
  51.0 5.9 %copy.23 = f32[4,512,512]{1,2,0:T(8,128)} copy(f32[4,512,512]{2,1,0:T(8,128)} %param.16) | data formatting | bytes 8388608 | tf_op args[7]
  56.9 24.3 %collective-permute-done.2 = bf16[512,512]{1,0:T(8,128)(2,1)} collective-permute-done((bf16[512,512]{1,0:T(8,128)(2,1)S(1)}, bf16[512,512]{1,0:T(8,128)(2,1)}, u32[]{:S(2)}, u32[]{:S(2)}) %collective-permute-start.2) | collective-permute-done | bytes 524320 | tf_op jit(solution)/shard_map/ppermute | solution.py:13
  82.4 17.1 %collective-permute-done = bf16[16,512,64]{1,2,0:T(8,128)(2,1)S(1)} collective-permute-done((bf16[16,512,64]{1,2,0:T(8,128)(2,1)}, bf16[16,512,64]{1,2,0:T(8,128)(2,1)S(1)}, u32[]{:S(2)}, u32[]{:S(2)}) %collective-permute-start) | collective-permute-done | bytes 1048608 | tf_op jit(solution)/shard_map/ppermute | solution.py:21
  99.5 6.9 %pad_maximum_fusion = bf16[16,3072,64]{1,2,0:T(8,128)(2,1)} fusion(bf16[16,512,64]{1,2,0:T(8,128)(2,1)S(1)} %collective-permute-done.1, bf16[16,2048,64]{1,2,0:T(8,128)(2,1)} %bitcast.54, bf16[16,512,64]{1,2,0:T(8,128)(2,1)S(1)} %collective-permute-done), kind=kLoop, calls=%fused_computation.6 | loop fusion | flops 18874368 | bytes 12582912 | tf_op jit(solution)/shard_map/concatenate | solution.py:25
  106.4 13.6 %reshape.74 = bf16[16,6,512,64]{2,1,3,0:T(8,128)(2,1)} reshape(bf16[16,3072,64]{1,2,0:T(8,128)(2,1)} %pad_maximum_fusion) | data formatting | bytes 12582912 | tf_op jit(solution)/shard_map/reshape | solution.py:54
  120.0 14.8 %fusion.42 = (bf16[16,4,512,64]{2,1,3,0:T(4,128)(2,1)}, bf16[16,4,512,64]{2,1,3,0:T(4,128)(2,1)S(1)}, bf16[16,4,512,64]{2,1,3,0:T(4,128)(2,1)S(1)}) fusion(bf16[16,6,512,64]{2,1,3,0:T(8,128)(2,1)} %reshape.74), kind=kLoop, calls=%fused_computation.60 | loop fusion | bytes 25165824 | tf_op jit(solution)/shard_map/slice | solution.py:57
  134.8 9.1 %fusion.7 = f32[4,16,64,512]{3,2,1,0:T(8,128)} fusion(bf16[16,4,512,64]{2,1,3,0:T(4,128)(2,1)S(1)} %get-tuple-element.7, f32[4,512,512]{2,1,0:T(8,128)S(1)} %copy-done.4), kind=kOutput, calls=%fused_computation.14 | convolution fusion | flops 12884901888 | bytes 16777216 | tf_op jit(solution)/shard_map/bij,pbjc->pbic/dot_general | solution.py:61
  143.9 9.4 %fusion.10 = f32[4,16,64,512]{3,2,1,0:T(8,128)} fusion(f32[4,512,512]{2,1,0:T(8,128)S(1)} %copy-done.2, f32[4,512,512]{1,2,0:T(8,128)S(1)} %copy-done.3, bf16[16,4,512,64]{2,1,3,0:T(4,128)(2,1)S(1)} %get-tuple-element.8), kind=kOutput, calls=%fused_computation.17 | convolution fusion | flops 12886999040 | bytes 20971520 | tf_op jit(solution)/shard_map/bij,pbjc->pbic/dot_general | solution.py:60
  153.3 16.3 %fusion = f32[4,16,8,8,512]{4,3,2,1,0:T(8,128)} fusion(f32[4,16,64,512]{3,2,1,0:T(8,128)} %fusion.10, f32[4,16,64,512]{3,2,1,0:T(8,128)} %fusion.7, f32[4,512]{1,0:T(4,128)S(1)} %mul.78, bf16[16,4,512,64]{2,1,3,0:T(4,128)(2,1)S(1)} %get-tuple-element.8, f32[1,512,512]{2,1,0:T(8,128)S(1)} %bitcast_convert_fusion, f32[3,512,512]{2,1,0:T(8,128)S(1)} %slice-done, ...), kind=kOutput, calls=%fused_computation.1 | convolution fusion | flops 12896436224 | bytes 37756928 | tf_op jit(solution)/shard_map/bji,pbjc->pbic/dot_general | solution.py:64
  169.6 8.2 %copy.35 = f32[4,16,8,8,512]{4,3,0,2,1:T(8,128)} copy(f32[4,16,8,8,512]{4,3,2,1,0:T(8,128)} %fusion) | data formatting | bytes 16777216 | tf_op jit(solution)/shard_map/reshape | solution.py:66
  177.9 10.6 %fusion.44 = f32[16,256,64]{1,2,0:T(8,128)} fusion(bf16[16,2048,256]{1,2,0:T(8,128)(2,1)} %all-gather.2.cloned.1.call-done, bf16[16,2048,64]{1,2,0:T(8,128)(2,1)} %bitcast.55), kind=kOutput, calls=%fused_computation.62 | convolution fusion | flops 1073741824 | bytes 22020096 | tf_op jit(solution)/shard_map/pri,prj->pij/dot_general | solution.py:101
  188.5 20.9 %fusion.45 = f32[16,256,64]{1,2,0:T(8,128)} fusion(bf16[16,2048,256]{1,2,0:T(8,128)(2,1)} %all-gather.2.cloned.1.call-done, f32[16,2048,64]{1,2,0:T(8,128)} %bitcast.58), kind=kOutput, calls=%fused_computation.63 | convolution fusion | flops 6442450944 | bytes 26214400 | tf_op jit(solution)/shard_map/pri,prj->pij/dot_general | solution.py:102
  209.5 102.9 %all-reduce.3.cloned.1.call-done = (f32[16,256,64]{1,2,0:T(8,128)}, f32[16,256,64]{1,2,0:T(8,128)}) async-done(((f32[16,256,64]{1,2,0:T(8,128)}, f32[16,256,64]{1,2,0:T(8,128)}), (f32[16,256,64]{1,2,0:T(8,128)}, f32[16,256,64]{1,2,0:T(8,128)})) %all-reduce.3.cloned.1.call-update) | async-done | bytes 2097168 | tf_op jit(solution)/shard_map/psum | solution.py:103
  312.5 1.9 select_reduce_fusion.1
  314.4 16.1 %multiply_reduce_fusion = (f32[16,64]{1,0:T(8,128)S(1)}, f32[16,2048,64]{1,2,0:T(8,128)}) fusion(bf16[16,2048,64]{1,2,0:T(8,128)(2,1)} %bitcast.56, bf16[16,2048,256]{1,2,0:T(8,128)(2,1)} %all-gather.2.cloned.1.call-done, f32[16,256,64]{1,2,0:T(8,128)} %get-tuple-element.4, f32[16,256,64]{1,2,0:T(8,128)} %get-tuple-element.5, ...), kind=kOutput, calls=%fused_computation.2 | convolution fusion | flops 6452935680 | bytes 31563776 | tf_op jit(solution)/shard_map/pri,pij->prj/dot_general | solution.py:112
  330.5 20.3 %psum.31 = f32[16,64]{1,0:T(8,128)S(1)} all-reduce(f32[16,64]{1,0:T(8,128)S(1)} %get-tuple-element.13), channel_id=1, replica_groups=mesh['row'=8,'col'=4] {'row'}, use_global_device_ids=true, to_apply=%region_6.7 | all-reduce | flops 1024 | bytes 8192 | tf_op jit(solution)/shard_map/psum | solution.py:113
  351.4 9.0 %fusion.1 = f32[16,2048,64]{1,2,0:T(8,128)} fusion(f32[16,2048,64]{1,2,0:T(8,128)} %get-tuple-element.14, bf16[16,2048,64]{1,2,0:T(8,128)(2,1)} %bitcast.57, f32[16,64]{1,0:T(8,128)S(1)} %divide_sqrt_fusion), kind=kLoop, calls=%fused_computation.7 | loop fusion | flops 6291456 | bytes 20975616 | tf_op jit(solution)/shard_map/mul | solution.py:115
  (34 shorter events, 7.8 us)
Async XLA Ops:
  7.2 29.5 %copy-start = (bf16[4,512,512]{2,1,0:T(8,128)(2,1)S(1)}, bf16[4,512,512]{2,1,0:T(8,128)(2,1)}, u32[]{:S(2)}) copy-start(bf16[4,512,512]{2,1,0:T(8,128)(2,1)} %param.15) | copy-start | bytes 6291460
  7.2 170.7 %all-gather.2.cloned.1.call-start = ((), (), s32[]{:S(2)}) async-start(), calls=%async_computation | async-start | bytes 20971520 | tf_op jit(solution)/shard_map/all_gather | solution.py:95
  42.0 270.4 %all-reduce.3.cloned.1.call-start = ((), (), s32[]{:S(2)}) async-start(), calls=%async_computation.1 | async-start | bytes 4194304 | tf_op jit(solution)/shard_map/psum | solution.py:103
  45.2 54.2 %collective-permute-start = (bf16[16,512,64]{1,2,0:T(8,128)(2,1)}, bf16[16,512,64]{1,2,0:T(8,128)(2,1)S(1)}, u32[]{:S(2)}, u32[]{:S(2)}) collective-permute-start(bf16[16,512,64]{1,2,0:T(8,128)(2,1)} %get-tuple-element.9), channel_id=1, source_target_pairs={{0,4},{4,8},{8,12},{12,16},{16,20},{20,24},{24,28},{1,5},{5,9},{9,... | collective-permute-start | bytes 3145736 | tf_op jit(solution)/shard_map/ppermute | solution.py:21
  46.6 52.9 %collective-permute-start.1 = (bf16[16,512,64]{1,2,0:T(8,128)(2,1)}, bf16[16,512,64]{1,2,0:T(8,128)(2,1)S(1)}, u32[]{:S(2)}, u32[]{:S(2)}) collective-permute-start(bf16[16,512,64]{1,2,0:T(8,128)(2,1)} %get-tuple-element.10), channel_id=1, source_target_pairs={{4,0},{8,4},{12,8},{16,12},{20,16},{24,20},{28,24},{5,1},{9,5},{13... | collective-permute-start | bytes 3145736 | tf_op jit(solution)/shard_map/ppermute | solution.py:24
  49.4 7.5 %copy-start.5 = (f32[2048]{0:T(1024)S(1)}, f32[2048]{0:T(1024)}, u32[]{:S(2)}) copy-start(f32[2048]{0:T(1024)} %param.12) | copy-start | bytes 24580
  49.4 31.8 %collective-permute-start.2 = (bf16[512,512]{1,0:T(8,128)(2,1)S(1)}, bf16[512,512]{1,0:T(8,128)(2,1)}, u32[]{:S(2)}, u32[]{:S(2)}) collective-permute-start(bf16[512,512]{1,0:T(8,128)(2,1)S(1)} %fusion.32), channel_id=1, source_target_pairs={{4,0},{8,4},{12,8},{16,12},{20,16},{24,20},{28,24},{5,1},{9,5},{13... | collective-permute-start | bytes 1572872 | tf_op jit(solution)/shard_map/ppermute | solution.py:13
  120.0 14.8 %copy-start.4 = (f32[4,512,512]{2,1,0:T(8,128)S(1)}, f32[4,512,512]{2,1,0:T(8,128)}, u32[]{:S(2)}) copy-start(f32[4,512,512]{2,1,0:T(8,128)} %param.17) | copy-start | bytes 12582916
  134.8 9.1 %copy-start.2 = (f32[4,512,512]{2,1,0:T(8,128)S(1)}, f32[4,512,512]{2,1,0:T(8,128)}, u32[]{:S(2)}) copy-start(f32[4,512,512]{2,1,0:T(8,128)} %param.16) | copy-start | bytes 12582916
  134.8 9.1 %copy-start.3 = (f32[4,512,512]{1,2,0:T(8,128)S(1)}, f32[4,512,512]{1,2,0:T(8,128)}, u32[]{:S(2)}) copy-start(f32[4,512,512]{1,2,0:T(8,128)} %copy.23) | copy-start | bytes 12582916
  143.9 9.4 %slice-start = ((f32[4,512,512]{2,1,0:T(8,128)}), f32[3,512,512]{2,1,0:T(8,128)S(1)}, s32[]{:S(2)}) async-start(f32[4,512,512]{2,1,0:T(8,128)} %param.17), calls=%async_computation.2 | async-start | bytes 6291456 | tf_op jit(solution)/shard_map/slice | solution.py:58
  351.4 9.0 %copy-start.1 = (bf16[4,512,512]{2,1,0:T(8,128)(2,1)S(1)}, bf16[4,512,512]{2,1,0:T(8,128)(2,1)}, u32[]{:S(2)}) copy-start(bf16[4,512,512]{2,1,0:T(8,128)(2,1)} %param.15) | copy-start | bytes 6291460
Sparse Core Ops, SparseCore 0:
  42.2 103.2 all-gather.1
  209.5 102.8 all-reduce.2
where the time goes:
time: 368 us; the launch traced here: 367 us
  waiting for transfers between devices  144 us (39%)
  matrix products  85.2 us (23%)
  local copies, waits for them, and re-layouts  50.7 us (14%)
  blocking collectives  43.6 us (12%)
  other arithmetic  24.9 us (7%)
  between operations  14.2 us (4%)
  starting transfers between devices  4.32 us (1%)
    psum x1, waiting for transfers between devices, shards(): gram, projected = lax.psum((gram, projected), 'row')  103 us
    ppermute x1, waiting for transfers between devices, from_behind(): lax.ppermute(value, axis, [(source, source + steps) for source in range(i...  24.3 us
    psum x1, blocking collectives, form_panel(): column_squares = lax.psum(jnp.sum(cauchy * cauchy, axis=1), 'row')  23.3 us
    dot_general x1, matrix products, shards(): jnp.einsum('pri,prj->pij', all_float, operated, precision=HIGHEST)  20.9 us
    psum x1, blocking collectives, shards(): column_sums = lax.psum(jnp.sum(updated * updated, axis=1), 'row')  20.3 us
    ppermute x1, waiting for transfers between devices, with_halo(): lax.ppermute(lax.slice_in_dim(block, block.shape[dim] - width, None, axis...  17.1 us
    dot_general x1, matrix products, apply_operator(): jnp.einsum('bji,pbjc->pbic', upper_blocks, upper_rows, precision=HIGHEST)  16.3 us
    dot_general x1, matrix products, shards(): jnp.einsum('pri,pij->prj', all_float, update, precision=HIGHEST)  16.1 us
  transfers between devices with their start and end apart: 5, of which 3 were waited for; matrix products, arithmetic and copies ran while one was open for 25% of the time, Pallas kernels for 0%

commit v1 on v0

v1 whole, which is shorter than its diff:
```python
import functools

import jax
import jax.numpy as jnp
from jax import lax
from jax.experimental import pallas as pl
from jax.experimental.pallas import tpu as pltpu
from jax.sharding import PartitionSpec as P

EPSILON = 1e-06
HIGHEST = lax.Precision.HIGHEST
MESH = pl.DeviceIdType.MESH
LANES = 128


def dot_nt(a, b):
    return lax.dot_general(a, b, (((1,), (1,)), ((), ())), preferred_element_type=jnp.float32)


def split(x):
    high = x.astype(jnp.bfloat16)
    return high, (x - high.astype(jnp.float32)).astype(jnp.bfloat16)


def widen(x, width):
    return jnp.concatenate([x] * (width // x.shape[1]), axis=1)


def column_form(row):
    return jnp.transpose(jnp.broadcast_to(row, (LANES, row.shape[1])))


def merge_kernel(
    rows,
    cols,
    pole_ref,
    rank_ref,
    defl_ref,
    onsite_ref,
    chosen_ref,
    chosen_col_ref,
    q_ref,
    diag_ref,
    coup_ref,
    formed_hbm,
    update_out,
    pw,
    halo_pw,
    halo_q,
    sq_send,
    sq_slots,
    factor_col,
    hmat,
    formed,
    halo,
    sums_send,
    sums_slots,
    v_full,
    v_send,
    out_sem,
    halo_send_sem,
    halo_recv_sem,
    sq_send_sem,
    sq_recv_sem,
    sums_send_sem,
    sums_recv_sem,
    v_send_sem,
    v_recv_sem,
):
    row = lax.axis_index("row")
    col = lax.axis_index("col")
    me = row * cols + col
    total = rows * cols
    panels, size = chosen_ref.shape
    own = panels // cols
    block_count, block, _ = q_ref.shape
    here = block_count * block
    width = size // cols
    spread = rows // own

    barrier = pltpu.get_barrier_semaphore()

    def greet(step, carry):
        other = lax.rem(me + step, total)
        pl.semaphore_signal(
            barrier, inc=1, device_id=(other // cols, lax.rem(other, cols)), device_id_type=MESH
        )
        return carry

    lax.fori_loop(1, total, greet, 0)

    weights = rank_ref[...] * (1 - defl_ref[...]).astype(jnp.float32)
    pw[0:8, :] = jnp.broadcast_to(pole_ref[...], (8, here))
    pw[8:16, :] = jnp.broadcast_to(weights, (8, here))

    def cauchy_of(poles, weight_row, panel):
        chosen = widen(chosen_col_ref[panel], poles.shape[1])
        return weight_row / (poles - chosen)

    sq_send[...] = jnp.zeros_like(sq_send)
    for k in range(own):

        def add_squares(b, acc):
            lanes = pl.ds(pl.multiple_of(b * block, block), block)
            c = cauchy_of(pw[0:1, lanes], pw[8:9, lanes], col * own + k)
            c = c * c
            for t in range(block // LANES):
                acc = acc + c[:, t * LANES : (t + 1) * LANES]
            return acc

        acc = lax.fori_loop(0, block_count, add_squares, jnp.zeros((size, LANES), jnp.float32))
        sq_send[k : k + 1, :] = jnp.sum(jnp.transpose(acc), axis=0, keepdims=True)

    pl.semaphore_wait(barrier, total - 1)

    last = block_count - 1
    tail = pl.ds(here - block, block)
    halo_copies = [
        pltpu.make_async_remote_copy(
            src_ref=source,
            dst_ref=target,
            send_sem=halo_send_sem.at[n],
            recv_sem=halo_recv_sem.at[n],
            device_id=(lax.rem(row + 1, rows), col),
            device_id_type=MESH,
        )
        for n, (source, target) in enumerate(((q_ref.at[last], halo_q), (pw.at[:, tail], halo_pw)))
    ]

    def square_copy(step):
        other = lax.rem(me + step, total)
        return pltpu.make_async_remote_copy(
            src_ref=sq_send,
            dst_ref=sq_slots.at[me],
            send_sem=sq_send_sem.at[step],
            recv_sem=sq_recv_sem.at[me],
            device_id=(other // cols, lax.rem(other, cols)),
            device_id_type=MESH,
        )

    def send_squares(step, carry):
        square_copy(step).start()
        return carry

    lax.fori_loop(1, total, send_squares, 0)

    @pl.when(row < rows - 1)
    def _():
        for copy in halo_copies:
            copy.start()

    sq_slots[me] = sq_send[...]

    for b in range(block_count):
        for n, part in enumerate((coup_ref[b], 0.5 * diag_ref[b])):
            high, low = split(part)
            hmat[b, n, 0] = high
            hmat[b, n, 1] = low

    def await_squares(step, carry):
        other = lax.rem(me + step, total)
        square_copy(step).wait_send()
        pltpu.make_async_remote_copy(
            src_ref=sq_send,
            dst_ref=sq_slots.at[other],
            send_sem=sq_send_sem.at[step],
            recv_sem=sq_recv_sem.at[other],
            device_id=(other // cols, lax.rem(other, cols)),
            device_id_type=MESH,
        ).wait_recv()
        return carry

    lax.fori_loop(1, total, await_squares, 0)

    for c in range(cols):
        sums = lax.fori_loop(
            0, rows, lambda r, a: a + sq_slots[r * cols + c], jnp.zeros(sq_send.shape, jnp.float32)
        )
        factor = lax.rsqrt(sums + EPSILON)
        for k in range(own):
            factor_col[c * own + k] = column_form(factor[k : k + 1, :])

    def form_block(poles, weight_row, panel, q_block):
        scaled = cauchy_of(poles, weight_row, panel) * widen(factor_col[panel], block)
        return dot_nt(scaled.astype(jnp.bfloat16), q_block).astype(jnp.bfloat16)

    def form_panel(panel):
        for b in range(block_count):
            lanes = pl.ds(b * block, block)
            formed[panel, :, lanes] = form_block(pw[0:1, lanes], pw[8:9, lanes], panel, q_ref[b])
        out_copy(panel).start()

    def out_copy(panel):
        return pltpu.make_async_copy(formed.at[panel], formed_hbm.at[panel], out_sem.at[panel])

    i_at = lax.broadcasted_iota(jnp.int32, (size, size), 0)
    j_at = lax.broadcasted_iota(jnp.int32, (size, size), 1)

    @pl.when(row > 0)
    def _():
        for copy in halo_copies:
            copy.wait_recv()

    def owner_row(k):
        return k * spread + lax.rem(col, spread)

    def sums_copy(k):
        return pltpu.make_async_remote_copy(
            src_ref=sums_send.at[k],
            dst_ref=sums_slots.at[row],
            send_sem=sums_send_sem.at[k],
            recv_sem=sums_recv_sem.at[row],
            device_id=(owner_row(k), col),
            device_id_type=MESH,
        )

    def own_panel(k, carry):
        panel = col * own + k
        form_panel(panel)

        @pl.when(row > 0)
        def _():
            halo[...] = form_block(halo_pw[0:1, :], halo_pw[8:9, :], panel, halo_q[...])

        @pl.when(row == 0)
        def _():
            halo[...] = jnp.zeros_like(halo)

        gram = jnp.zeros((size, size), jnp.float32)
        half = jnp.zeros((size, size), jnp.float32)
        for b in range(block_count):
            lanes = pl.ds(b * block, block)
            now = formed[panel, :, lanes]
            before = halo[...] if b == 0 else formed[panel, :, pl.ds((b - 1) * block, block)]
            image = dot_nt(before, hmat[b, 0, 0]) + dot_nt(before, hmat[b, 0, 1])
            image = image + dot_nt(now, hmat[b, 1, 0]) + dot_nt(now, hmat[b, 1, 1])
            image = image + 0.5 * onsite_ref[0:1, lanes] * now.astype(jnp.float32)
            high, low = split(image)
            gram = gram + dot_nt(now, now)
            half = half + dot_nt(now, high) + dot_nt(now, low)
        projected = half + jnp.transpose(half)
        sums_send[k, 0:size, :] = jnp.where(j_at > i_at, gram, projected)
        diagonal = jnp.sum(jnp.where(i_at == j_at, gram, 0.0), axis=0, keepdims=True)
        sums_send[k, size : size + 8, :] = jnp.broadcast_to(diagonal, (8, size))

        @pl.when(owner_row(k) != row)
        def _():
            sums_copy(k).start()

        @pl.when(owner_row(k) == row)
        def _():
            sums_slots[row] = sums_send[k]

        return carry

    lax.fori_loop(0, own, own_panel, 0)

    def rest(n, carry):
        form_panel(lax.rem(col * own + own + n, panels))
        return carry

    lax.fori_loop(0, panels - own, rest, 0)

    mine = row // spread
    owns = owner_row(mine) == row

    def update_copy(step):
        other = lax.rem(me + step, total)
        other_col = lax.rem(other, cols)
        return pltpu.make_async_remote_copy(
            src_ref=v_send.at[other_col],
            dst_ref=update_out.at[col * own + mine],
            send_sem=v_send_sem.at[step],
            recv_sem=v_recv_sem.at[col * own + mine],
            device_id=(other // cols, other_col),
            device_id_type=MESH,
        )

    @pl.when(owns)
    def _():
        panel = col * own + mine

        def arrive(step, carry):
            other = lax.rem(row + step, rows)
            pltpu.make_async_remote_copy(
                src_ref=sums_send.at[0],
                dst_ref=sums_slots.at[other],
                send_sem=sums_send_sem.at[0],
                recv_sem=sums_recv_sem.at[other],
                device_id=(other, col),
                device_id_type=MESH,
            ).wait_recv()
            return carry

        lax.fori_loop(1, rows, arrive, 0)
        sums = lax.fori_loop(
            1, rows, lambda r, a: a + sums_slots[r], sums_slots[0]
        )
        packed = sums[0:size, :]
        diagonal = sums[size : size + 1, :]
        turned = jnp.transpose(packed)
        on_diagonal = i_at == j_at
        identity = jnp.where(on_diagonal, 1.0, 0.0)
        gram = jnp.where(j_at > i_at, packed, jnp.where(on_diagonal, diagonal, turned))
        projected = jnp.where(j_at > i_at, turned, packed)
        residual = identity - gram
        right = chosen_ref[pl.ds(panel, 1), :]
        left = widen(chosen_col_ref[panel], size)
        spacing = right - left + identity
        update = jnp.where(
            on_diagonal, 0.5 * residual, (projected + right * residual) / spacing
        )
        v = identity + update
        gv = jnp.dot(gram, v, precision=HIGHEST, preferred_element_type=jnp.float32)
        column_sums = jnp.sum(v * gv, axis=0, keepdims=True)
        matrix_order = float(here * rows)
        v = v * jnp.sqrt(matrix_order / column_sums)
        v_full[...] = jnp.transpose(v)
        new_roots = (
            jnp.sum(jnp.where(on_diagonal, projected, 0.0), axis=0, keepdims=True) / diagonal
        )
        for c in range(cols):
            v_send[c, 0:width, :] = v_full[c * width : (c + 1) * width, :]
            v_send[c, width : width + 8, :] = jnp.broadcast_to(new_roots, (8, size))

        def send_update(step, carry):
            update_copy(step).start()
            return carry

        lax.fori_loop(1, total, send_update, 0)
        update_out[panel] = v_send[col]

    for c in range(cols):
        for k in range(own):
            from_row = k * spread + c % spread

            @pl.when(jnp.logical_or(row != from_row, col != c))
            def _():
                pltpu.make_async_remote_copy(
                    src_ref=v_send.at[0],
                    dst_ref=update_out.at[c * own + k],
                    send_sem=v_send_sem.at[0],
                    recv_sem=v_recv_sem.at[c * own + k],
                    device_id=(from_row, c),
                    device_id_type=MESH,
                ).wait_recv()

    @pl.when(owns)
    def _():
        def sent(step, carry):
            update_copy(step).wait_send()
            return carry

        lax.fori_loop(1, total, sent, 0)

    for k in range(own):

        @pl.when(owner_row(k) != row)
        def _():
            sums_copy(k).wait_send()

    @pl.when(row < rows - 1)
    def _():
        for copy in halo_copies:
            copy.wait_send()

    def written(panel, carry):
        out_copy(panel).wait()
        return carry

    lax.fori_loop(0, panels, written, 0)


def finish_kernel(width, v_ref, formed_ref, out_ref):
    high, low = split(v_ref[0, 0:width, :])
    parts = jnp.dot(
        jnp.concatenate([high, low], axis=0), formed_ref[0], preferred_element_type=jnp.float32
    )
    out_ref[0] = parts[0:width] + parts[width : 2 * width]


def pick_roots(secular_roots, column_order):
    panel_slots = jnp.arange(secular_roots.shape[1], dtype=jnp.int32)
    selector = (column_order[:, :, None] == panel_slots[None, None, :]).astype(jnp.float32)
    return jnp.sum(selector * secular_roots[:, None, :], axis=2)


def shards(
    pole_values,
    rank_one,
    deflated,
    onsite_energy,
    secular_roots,
    column_order,
    q_blocks,
    diag_blocks,
    coupling_blocks,
):
    rows, cols = lax.axis_size("row"), lax.axis_size("col")
    here = pole_values.shape[0]
    panels, size = secular_roots.shape
    block_count, block, _ = q_blocks.shape
    width = size // cols
    own = panels // cols
    total = rows * cols
    own_pad = -(-own // 8) * 8
    chosen = pick_roots(secular_roots, column_order)
    chosen_col = jnp.broadcast_to(chosen[:, :, None], (panels, size, LANES))
    vmem = pl.BlockSpec(memory_space=pltpu.VMEM)
    f32, bf16 = jnp.float32, jnp.bfloat16
    dma = pltpu.SemaphoreType.DMA
    formed, update = pl.pallas_call(
        functools.partial(merge_kernel, rows, cols),
        out_shape=(
            jax.ShapeDtypeStruct((panels, size, here), bf16),
            jax.ShapeDtypeStruct((panels, width + 8, size), f32),
        ),
        in_specs=[vmem] * 9,
        out_specs=(pl.BlockSpec(memory_space=pl.ANY), vmem),
        scratch_shapes=[
            pltpu.VMEM((16, here), f32),
            pltpu.VMEM((16, block), f32),
            pltpu.VMEM((block, block), bf16),
            pltpu.VMEM((own_pad, size), f32),
            pltpu.VMEM((total, own_pad, size), f32),
            pltpu.VMEM((panels, size, LANES), f32),
            pltpu.VMEM((block_count, 2, 2, block, block), bf16),
            pltpu.VMEM((panels, size, here), bf16),
            pltpu.VMEM((size, block), bf16),
            pltpu.VMEM((own, size + 8, size), f32),
            pltpu.VMEM((rows, size + 8, size), f32),
            pltpu.VMEM((size, size), f32),
            pltpu.VMEM((cols, width + 8, size), f32),
            dma((panels,)),
            dma((2,)),
            dma((2,)),
            dma((total,)),
            dma((total,)),
            dma((own,)),
            dma((rows,)),
            dma((total,)),
            dma((panels,)),
        ],
        compiler_params=pltpu.CompilerParams(
            collective_id=0, has_side_effects=True, vmem_limit_bytes=60 * 2**20
        ),
        name="merge",
    )(
        pole_values.reshape(1, here),
        rank_one.reshape(1, here),
        deflated.reshape(1, here),
        onsite_energy.reshape(1, here),
        chosen,
        chosen_col,
        q_blocks,
        diag_blocks,
        coupling_blocks,
    )
    refined = pl.pallas_call(
        functools.partial(finish_kernel, width),
        grid=(panels,),
        out_shape=jax.ShapeDtypeStruct((panels, width, here), f32),
        in_specs=[
            pl.BlockSpec((1, width + 8, size), lambda p: (p, 0, 0)),
            pl.BlockSpec((1, size, here), lambda p: (p, 0, 0)),
        ],
        out_specs=pl.BlockSpec((1, width, here), lambda p: (p, 0, 0)),
        compiler_params=pltpu.CompilerParams(vmem_limit_bytes=32 * 2**20),
        name="finish",
    )(update, formed)
    new_roots = lax.dynamic_slice_in_dim(
        update[:, width, :], lax.axis_index("col") * width, width, 1
    )
    return (jnp.swapaxes(refined, 1, 2), new_roots)


def solution(mesh):
    placed = (
        P("row"),
        P("row"),
        P("row"),
        P("row"),
        P(),
        P(),
        P("row", None, None),
        P("row", None, None),
        P("row", None, None),
    )
    return jax.shard_map(
        shards,
        mesh=mesh,
        in_specs=placed,
        out_specs=(P(None, "row", "col"), P(None, "col")),
        check_vma=False,
    )
```

time: 368 us -> 128 us (0.35)
  the two profiles are of different devices: /device:TPU:0 before, /device:TPU:23 now
where the time goes in v1:
time: 128 us
  Pallas kernels  115 us (90%)
  local copies, waits for them, and re-layouts  9.66 us (8%)
  other arithmetic  2.01 us (2%)
    pallas_call x1, Pallas kernels, shards(): pl.pallas_call(functools.partial(merge_kernel, rows, cols), out_shape=(ja...  106 us
    pallas_call x1, Pallas kernels, shards(): pl.pallas_call(functools.partial(finish_kernel, width), grid=(panels,), o...  9.16 us
    unnamed x6, local copies, waits for them, and re-layouts  7.04 us

profile of v1, /device:TPU:23, one launch (start us, length us, event | category | flops | bytes accessed | tf_op | source)
XLA Modules:
  0.0 127.8 jit_solution(8259072656384061231)
XLA Ops:
  0.6 2.0 %select_reduce_fusion.chosen_ref = f32[16,256]{1,0:T(8,128)S(1)} fusion(f32[16,256]{1,0:T(8,128)} %param.13, s32[16,256]{1,0:T(8,128)} %param.14), kind=kLoop, calls=%fused_computation | loop fusion | flops 3141632 | bytes 49152 | tf_op jit(solution)/shard_map/reduce_sum | solution.py:385
  2.6 0.0 copy-start.2
  2.7 1.9 %broadcast_in_dim.2.chosen_col_ref = f32[16,256,128]{2,1,0:T(8,128)} broadcast(f32[16,256]{1,0:T(8,128)S(1)} %select_reduce_fusion.chosen_ref), dimensions={0,1} | broadcast | bytes 2113536 | tf_op jit(solution)/shard_map/broadcast_in_dim | solution.py:408
  4.6 0.0 copy-done.2
  4.6 106.3 %merge.1 = (bf16[16,256,2048]{2,1,0:T(8,128)(2,1)}, f32[16,72,256]{2,1,0:T(8,128)}) custom-call(f32[1,2048]{1,0:T(1,128)} %bitcast.7, f32[1,2048]{1,0:T(1,128)} %bitcast.8, s32[1,2048]{1,0:T(1,128)} %bitcast.9, f32[1,2048]{1,0:T(1,128)} %bitcast.10, f32[16,256]{1,0:T(8,128)} %copy-done.2, f32[16,256,128]{2,1,0:T(8,128)} %broadcast_in_dim.2.chosen_col_ref, ...), custom_call_target="tpu_custom_call" | custom-call | tf_op jit(solution)/shard_map/merge/pallas_call | solution.py:412
  110.9 0.0 copy-start
  110.9 5.8 %copy-done = bf16[16,256,2048]{2,1,0:T(8,128)(2,1)S(1)} copy-done((bf16[16,256,2048]{2,1,0:T(8,128)(2,1)S(1)}, bf16[16,256,2048]{2,1,0:T(8,128)(2,1)}, u32[]{:S(2)}) %copy-start) | copy-done | bytes 16777240
  116.6 0.0 copy-start.1
  116.6 1.3 copy-done.1
  117.9 9.2 %finish.1 = f32[16,64,2048]{2,1,0:T(8,128)} custom-call(f32[16,72,256]{2,1,0:T(8,128)S(1)} %copy-done.1, bf16[16,256,2048]{2,1,0:T(8,128)(2,1)S(1)} %copy-done), custom_call_target="tpu_custom_call" | custom-call | tf_op jit(solution)/shard_map/finish/pallas_call | solution.py:459
  127.1 0.7 constant_dynamic-slice_fusion
  (1 shorter events, 0.0 us)
Async XLA Ops:
  2.6 1.9 %copy-start.2 = (f32[16,256]{1,0:T(8,128)}, f32[16,256]{1,0:T(8,128)S(1)}, u32[]{:S(2)}) copy-start(f32[16,256]{1,0:T(8,128)S(1)} %select_reduce_fusion.chosen_ref) | copy-start | bytes 49156
  110.9 5.8 %copy-start = (bf16[16,256,2048]{2,1,0:T(8,128)(2,1)S(1)}, bf16[16,256,2048]{2,1,0:T(8,128)(2,1)}, u32[]{:S(2)}) copy-start(bf16[16,256,2048]{2,1,0:T(8,128)(2,1)} %get-tuple-element.5.formed_ref) | copy-start | bytes 50331652
  116.6 1.3 copy-start.1

commit v2 on v1

--- a/solution.py
+++ b/solution.py
@@ -37,13 +37,19 @@
     rank_ref,
     defl_ref,
     onsite_ref,
-    chosen_ref,
-    chosen_col_ref,
+    roots_ref,
+    order_ref,
+    q_hbm,
+    diag_hbm,
+    coup_hbm,
+    refined_hbm,
+    roots_out,
     q_ref,
     diag_ref,
     coup_ref,
-    formed_hbm,
+    chosen_col_ref,
     update_out,
+    stage,
     pw,
     halo_pw,
     halo_q,
@@ -57,6 +63,7 @@
     sums_slots,
     v_full,
     v_send,
+    in_sem,
     out_sem,
     halo_send_sem,
     halo_recv_sem,
@@ -71,13 +78,22 @@
     col = lax.axis_index("col")
     me = row * cols + col
     total = rows * cols
-    panels, size = chosen_ref.shape
+    panels, size = roots_ref.shape
     own = panels // cols
     block_count, block, _ = q_ref.shape
     here = block_count * block
     width = size // cols
     spread = rows // own
 
+    in_copies = [
+        pltpu.make_async_copy(source, target, in_sem.at[n])
+        for n, (source, target) in enumerate(
+            ((q_hbm, q_ref), (coup_hbm, coup_ref), (diag_hbm, diag_ref))
+        )
+    ]
+    for copy in in_copies:
+        copy.start()
+
     barrier = pltpu.get_barrier_semaphore()
 
     def greet(step, carry):
@@ -93,12 +109,30 @@
     pw[0:8, :] = jnp.broadcast_to(pole_ref[...], (8, here))
     pw[8:16, :] = jnp.broadcast_to(weights, (8, here))
 
+    i_at = lax.broadcasted_iota(jnp.int32, (size, size), 0)
+    j_at = lax.broadcasted_iota(jnp.int32, (size, size), 1)
+
+    def choose(panel, carry=0):
+        order = column_form(order_ref[pl.ds(panel, 1), :].astype(jnp.float32))
+        selector = jnp.where(widen(order, size) == j_at.astype(jnp.float32), 1.0, 0.0)
+        selector = selector.astype(jnp.bfloat16)
+        roots = column_form(roots_ref[pl.ds(panel, 1), :])
+        high, low = split(roots)
+        rest = (roots - high.astype(jnp.float32)) - low.astype(jnp.float32)
+        picked = [
+            jnp.dot(selector, part, preferred_element_type=jnp.float32)
+            for part in (high, low, rest.astype(jnp.bfloat16))
+        ]
+        chosen_col_ref[panel] = (picked[0] + picked[1]) + picked[2]
+        return carry
+
     def cauchy_of(poles, weight_row, panel):
         chosen = widen(chosen_col_ref[panel], poles.shape[1])
         return weight_row / (poles - chosen)
 
     sq_send[...] = jnp.zeros_like(sq_send)
     for k in range(own):
+        choose(col * own + k)
 
         def add_squares(b, acc):
             lanes = pl.ds(pl.multiple_of(b * block, block), block)
@@ -124,7 +158,7 @@
             device_id=(lax.rem(row + 1, rows), col),
             device_id_type=MESH,
         )
-        for n, (source, target) in enumerate(((q_ref.at[last], halo_q), (pw.at[:, tail], halo_pw)))
+        for n, (source, target) in enumerate(((q_hbm.at[last], halo_q), (pw.at[:, tail], halo_pw)))
     ]
 
     def square_copy(step):
@@ -151,11 +185,15 @@
 
     sq_slots[me] = sq_send[...]
 
+    lax.fori_loop(
+        own, panels, lambda n, carry: choose(lax.rem(col * own + n, panels), carry), 0
+    )
+    for copy in in_copies:
+        copy.wait()
+
     for b in range(block_count):
-        for n, part in enumerate((coup_ref[b], 0.5 * diag_ref[b])):
-            high, low = split(part)
-            hmat[b, n, 0] = high
-            hmat[b, n, 1] = low
+        hmat[b, 0] = coup_ref[b].astype(jnp.bfloat16)
+        hmat[b, 1] = (0.5 * diag_ref[b]).astype(jnp.bfloat16)
 
     def await_squares(step, carry):
         other = lax.rem(me + step, total)
@@ -188,13 +226,19 @@
         for b in range(block_count):
             lanes = pl.ds(b * block, block)
             formed[panel, :, lanes] = form_block(pw[0:1, lanes], pw[8:9, lanes], panel, q_ref[b])
-        out_copy(panel).start()
-
-    def out_copy(panel):
-        return pltpu.make_async_copy(formed.at[panel], formed_hbm.at[panel], out_sem.at[panel])
-
-    i_at = lax.broadcasted_iota(jnp.int32, (size, size), 0)
-    j_at = lax.broadcasted_iota(jnp.int32, (size, size), 1)
+
+    def form_group(group):
+        for b in range(block_count):
+            lanes = pl.ds(b * block, block)
+            scaled = [
+                cauchy_of(pw[0:1, lanes], pw[8:9, lanes], group * own + k)
+                * widen(factor_col[group * own + k], block)
+                for k in range(own)
+            ]
+            scaled = jnp.concatenate([part.astype(jnp.bfloat16) for part in scaled], axis=0)
+            result = dot_nt(scaled, q_ref[b]).astype(jnp.bfloat16)
+            for k in range(own):
+                formed[group * own + k, :, lanes] = result[k * size : (k + 1) * size]
 
     @pl.when(row > 0)
     def _():
@@ -232,8 +276,7 @@
             lanes = pl.ds(b * block, block)
             now = formed[panel, :, lanes]
             before = halo[...] if b == 0 else formed[panel, :, pl.ds((b - 1) * block, block)]
-            image = dot_nt(before, hmat[b, 0, 0]) + dot_nt(before, hmat[b, 0, 1])
-            image = image + dot_nt(now, hmat[b, 1, 0]) + dot_nt(now, hmat[b, 1, 1])
+            image = dot_nt(before, hmat[b, 0]) + dot_nt(now, hmat[b, 1])
             image = image + 0.5 * onsite_ref[0:1, lanes] * now.astype(jnp.float32)
             high, low = split(image)
             gram = gram + dot_nt(now, now)
@@ -255,11 +298,12 @@
 
     lax.fori_loop(0, own, own_panel, 0)
 
-    def rest(n, carry):
-        form_panel(lax.rem(col * own + own + n, panels))
-        return carry
-
-    lax.fori_loop(0, panels - own, rest, 0)
+    def form_rest(n, carry):
+        form_group(lax.rem(col + n, cols))
+        return carry
+
+    late = max(1, cols - 1)
+    lax.fori_loop(1, late, form_rest, 0)
 
     mine = row // spread
     owns = owner_row(mine) == row
@@ -304,7 +348,7 @@
         gram = jnp.where(j_at > i_at, packed, jnp.where(on_diagonal, diagonal, turned))
         projected = jnp.where(j_at > i_at, turned, packed)
         residual = identity - gram
-        right = chosen_ref[pl.ds(panel, 1), :]
+        right = jnp.transpose(chosen_col_ref[panel])[0:1, :]
         left = widen(chosen_col_ref[panel], size)
         spacing = right - left + identity
         update = jnp.where(
@@ -330,20 +374,47 @@
         lax.fori_loop(1, total, send_update, 0)
         update_out[panel] = v_send[col]
 
-    for c in range(cols):
-        for k in range(own):
-            from_row = k * spread + c % spread
-
-            @pl.when(jnp.logical_or(row != from_row, col != c))
-            def _():
-                pltpu.make_async_remote_copy(
-                    src_ref=v_send.at[0],
-                    dst_ref=update_out.at[c * own + k],
-                    send_sem=v_send_sem.at[0],
-                    recv_sem=v_recv_sem.at[c * own + k],
-                    device_id=(from_row, c),
-                    device_id_type=MESH,
-                ).wait_recv()
+    lax.fori_loop(late, cols, form_rest, 0)
+
+    def out_copy(n):
+        panel = lax.rem(n, cols) * own + n // cols
+        return pltpu.make_async_copy(
+            stage.at[lax.rem(n, own)], refined_hbm.at[panel], out_sem.at[lax.rem(n, own)]
+        )
+
+    def finish(n, carry):
+        c, k = lax.rem(n, cols), n // cols
+        panel = c * own + k
+        from_row = k * spread + lax.rem(c, spread)
+
+        @pl.when(jnp.logical_or(row != from_row, col != c))
+        def _():
+            pltpu.make_async_remote_copy(
+                src_ref=v_send.at[0],
+                dst_ref=update_out.at[panel],
+                send_sem=v_send_sem.at[0],
+                recv_sem=v_recv_sem.at[panel],
+                device_id=(from_row, c),
+                device_id_type=MESH,
+            ).wait_recv()
+
+        high, low = split(update_out[panel, 0:width, :])
+        parts = jnp.dot(
+            jnp.concatenate([high, low], axis=0),
+            formed[panel],
+            preferred_element_type=jnp.float32,
+        )
+        roots_out[panel] = update_out[panel, width : width + 8, :]
+
+        @pl.when(n >= own)
+        def _():
+            out_copy(n - own).wait()
+
+        stage[lax.rem(n, own)] = parts[0:width] + parts[width : 2 * width]
+        out_copy(n).start()
+        return carry
+
+    lax.fori_loop(0, panels, finish, 0)
 
     @pl.when(owns)
     def _():
@@ -364,25 +435,11 @@
         for copy in halo_copies:
             copy.wait_send()
 
-    def written(panel, carry):
-        out_copy(panel).wait()
-        return carry
-
-    lax.fori_loop(0, panels, written, 0)
-
-
-def finish_kernel(width, v_ref, formed_ref, out_ref):
-    high, low = split(v_ref[0, 0:width, :])
-    parts = jnp.dot(
-        jnp.concatenate([high, low], axis=0), formed_ref[0], preferred_element_type=jnp.float32
-    )
-    out_ref[0] = parts[0:width] + parts[width : 2 * width]
-
-
-def pick_roots(secular_roots, column_order):
-    panel_slots = jnp.arange(secular_roots.shape[1], dtype=jnp.int32)
-    selector = (column_order[:, :, None] == panel_slots[None, None, :]).astype(jnp.float32)
-    return jnp.sum(selector * secular_roots[:, None, :], axis=2)
+    def written(n, carry):
+        out_copy(n).wait()
+        return carry
+
+    lax.fori_loop(panels - own, panels, written, 0)
 
 
 def shards(
@@ -404,34 +461,40 @@
     own = panels // cols
     total = rows * cols
     own_pad = -(-own // 8) * 8
-    chosen = pick_roots(secular_roots, column_order)
-    chosen_col = jnp.broadcast_to(chosen[:, :, None], (panels, size, LANES))
     vmem = pl.BlockSpec(memory_space=pltpu.VMEM)
     f32, bf16 = jnp.float32, jnp.bfloat16
     dma = pltpu.SemaphoreType.DMA
-    formed, update = pl.pallas_call(
+    anywhere = pl.BlockSpec(memory_space=pl.ANY)
+    refined, new_roots = pl.pallas_call(
         functools.partial(merge_kernel, rows, cols),
         out_shape=(
-            jax.ShapeDtypeStruct((panels, size, here), bf16),
-            jax.ShapeDtypeStruct((panels, width + 8, size), f32),
+            jax.ShapeDtypeStruct((panels, width, here), f32),
+            jax.ShapeDtypeStruct((panels, 8, size), f32),
         ),
-        in_specs=[vmem] * 9,
-        out_specs=(pl.BlockSpec(memory_space=pl.ANY), vmem),
+        in_specs=[vmem] * 6 + [anywhere] * 3,
+        out_specs=(anywhere, vmem),
         scratch_shapes=[
+            pltpu.VMEM(q_blocks.shape, bf16),
+            pltpu.VMEM(diag_blocks.shape, f32),
+            pltpu.VMEM(coupling_blocks.shape, f32),
+            pltpu.VMEM((panels, size, LANES), f32),
+            pltpu.VMEM((panels, width + 8, size), f32),
+            pltpu.VMEM((own, width, here), f32),
             pltpu.VMEM((16, here), f32),
             pltpu.VMEM((16, block), f32),
             pltpu.VMEM((block, block), bf16),
             pltpu.VMEM((own_pad, size), f32),
             pltpu.VMEM((total, own_pad, size), f32),
             pltpu.VMEM((panels, size, LANES), f32),
-            pltpu.VMEM((block_count, 2, 2, block, block), bf16),
+            pltpu.VMEM((block_count, 2, block, block), bf16),
             pltpu.VMEM((panels, size, here), bf16),
             pltpu.VMEM((size, block), bf16),
             pltpu.VMEM((own, size + 8, size), f32),
             pltpu.VMEM((rows, size + 8, size), f32),
             pltpu.VMEM((size, size), f32),
             pltpu.VMEM((cols, width + 8, size), f32),
-            dma((panels,)),
+            dma((3,)),
+            dma((own,)),
             dma((2,)),
             dma((2,)),
             dma((total,)),
@@ -450,26 +513,14 @@
         rank_one.reshape(1, here),
         deflated.reshape(1, here),
         onsite_energy.reshape(1, here),
-        chosen,
-        chosen_col,
+        secular_roots,
+        column_order,
         q_blocks,
         diag_blocks,
         coupling_blocks,
     )
-    refined = pl.pallas_call(
-        functools.partial(finish_kernel, width),
-        grid=(panels,),
-        out_shape=jax.ShapeDtypeStruct((panels, width, here), f32),
-        in_specs=[
-            pl.BlockSpec((1, width + 8, size), lambda p: (p, 0, 0)),
-            pl.BlockSpec((1, size, here), lambda p: (p, 0, 0)),
-        ],
-        out_specs=pl.BlockSpec((1, width, here), lambda p: (p, 0, 0)),
-        compiler_params=pltpu.CompilerParams(vmem_limit_bytes=32 * 2**20),
-        name="finish",
-    )(update, formed)
     new_roots = lax.dynamic_slice_in_dim(
-        update[:, width, :], lax.axis_index("col") * width, width, 1
+        new_roots[:, 0, :], lax.axis_index("col") * width, width, 1
     )
     return (jnp.swapaxes(refined, 1, 2), new_roots)
 

time: 128 us -> 110 us (0.86)
  Pallas kernels: 115 us -> 99.5 us
  other arithmetic: 2.01 us -> 0 us
    pallas_call x1 -> x0, Pallas kernels: 9.16 us -> none  [shards(): pl.pallas_call(functools.partial(finish_kernel, width), grid=(panels,), o...]
    pallas_call x1, Pallas kernels: 106 us -> 99.5 us  [shards(): pl.pallas_call(functools.partial(merge_kernel, rows, cols), out_shape=(ja...]
    reduce_sum x1 -> x0, other arithmetic: 2.01 us -> none  [pick_roots(): return jnp.sum(selector * secular_roots[:, None, :], axis=2)]
    broadcast_in_dim x1 -> x0, local copies, waits for them, and re-layouts: 1.92 us -> none  [shards(): chosen_col = jnp.broadcast_to(chosen[:, :, None], (panels, size, LANES))]
    unnamed x6 -> x1, local copies, waits for them, and re-layouts: 7.04 us -> 7.89 us
where the time goes in v2:
time: 110 us
  Pallas kernels  99.5 us (90%)
  local copies, waits for them, and re-layouts  9.49 us (9%)
    pallas_call x1, Pallas kernels, shards(): pl.pallas_call(functools.partial(merge_kernel, rows, cols), out_shape=(ja...  99.5 us
    unnamed x1, local copies, waits for them, and re-layouts  7.89 us

profile of v2, /device:TPU:23, one launch (start us, length us, event | category | flops | bytes accessed | tf_op | source)
XLA Modules:
  0.0 109.7 jit_solution(3111560835239339650)
XLA Ops:
  0.6 99.5 %merge.1 = (f32[16,64,2048]{2,1,0:T(8,128)}, f32[16,8,256]{2,1,0:T(8,128)}) custom-call(f32[1,2048]{1,0:T(1,128)} %bitcast.7, f32[1,2048]{1,0:T(1,128)} %bitcast.8, s32[1,2048]{1,0:T(1,128)} %bitcast.9, f32[1,2048]{1,0:T(1,128)} %bitcast.10, f32[16,256]{1,0:T(8,128)} %roots_ref.1, s32[16,256]{1,0:T(8,128)} %order_ref.1, bf16[4,512,512]{2,1,0:T(8,128)(2,1)} %q_hbm.1, ...), custom_call_target="tpu_custom_call" | custom-call | tf_op jit(solution)/shard_map/merge/pallas_call | solution.py:468
  100.2 0.9 slice.3
  101.1 0.7 constant_dynamic-slice_fusion
  101.8 7.9 %copy.12 = f32[16,2048,64]{1,2,0:T(8,128)} copy(f32[16,2048,64]{1,2,0:T(8,128)} %bitcast.6) | data formatting | bytes 16777216

commit v3 on v2

--- a/solution.py
+++ b/solution.py
@@ -60,17 +60,22 @@
     formed,
     halo,
     sums_send,
+    plane_slots,
     sums_slots,
     v_full,
-    v_send,
+    relay,
     in_sem,
     out_sem,
     halo_send_sem,
     halo_recv_sem,
     sq_send_sem,
     sq_recv_sem,
+    plane_send_sem,
+    plane_recv_sem,
     sums_send_sem,
     sums_recv_sem,
+    relay_send_sem,
+    relay_recv_sem,
     v_send_sem,
     v_recv_sem,
 ):
@@ -84,6 +89,10 @@
     here = block_count * block
     width = size // cols
     spread = rows // own
+    sub = size // LANES
+    high_row, low_row = row // spread, lax.rem(row, spread)
+    collects = low_row == lax.rem(col, spread)
+    collector = high_row * spread + lax.rem(col, spread)
 
     in_copies = [
         pltpu.make_async_copy(source, target, in_sem.at[n])
@@ -143,7 +152,9 @@
             return acc
 
         acc = lax.fori_loop(0, block_count, add_squares, jnp.zeros((size, LANES), jnp.float32))
-        sq_send[k : k + 1, :] = jnp.sum(jnp.transpose(acc), axis=0, keepdims=True)
+        squares = jnp.sum(jnp.transpose(acc), axis=0, keepdims=True)
+        for t in range(sub):
+            sq_send[k * sub + t : k * sub + t + 1, :] = squares[:, t * LANES : (t + 1) * LANES]
 
     pl.semaphore_wait(barrier, total - 1)
 
@@ -216,7 +227,11 @@
         )
         factor = lax.rsqrt(sums + EPSILON)
         for k in range(own):
-            factor_col[c * own + k] = column_form(factor[k : k + 1, :])
+            factor_col[c * own + k] = column_form(
+                jnp.concatenate(
+                    [factor[k * sub + t : k * sub + t + 1, :] for t in range(sub)], axis=1
+                )
+            )
 
     def form_block(poles, weight_row, panel, q_block):
         scaled = cauchy_of(poles, weight_row, panel) * widen(factor_col[panel], block)
@@ -245,18 +260,38 @@
         for copy in halo_copies:
             copy.wait_recv()
 
-    def owner_row(k):
-        return k * spread + lax.rem(col, spread)
-
-    def sums_copy(k):
+    def plane_copy(k, source_low):
         return pltpu.make_async_remote_copy(
             src_ref=sums_send.at[k],
-            dst_ref=sums_slots.at[row],
+            dst_ref=plane_slots.at[k, source_low],
+            send_sem=plane_send_sem.at[k],
+            recv_sem=plane_recv_sem.at[k, source_low],
+            device_id=(collector, col),
+            device_id_type=MESH,
+        )
+
+    def sums_copy(k, source_high):
+        return pltpu.make_async_remote_copy(
+            src_ref=sums_send.at[k],
+            dst_ref=sums_slots.at[source_high],
             send_sem=sums_send_sem.at[k],
-            recv_sem=sums_recv_sem.at[row],
-            device_id=(owner_row(k), col),
+            recv_sem=sums_recv_sem.at[source_high],
+            device_id=(k * spread + low_row, col),
             device_id_type=MESH,
         )
+
+    def collect(k):
+        def add(step, carry):
+            other = lax.rem(low_row + step, spread)
+            plane_copy(k, other).wait_recv()
+            sums_send[k] += plane_slots[k, other]
+            return carry
+
+        lax.fori_loop(1, spread, add, 0)
+
+        @pl.when(high_row != k)
+        def _():
+            sums_copy(k, high_row).start()
 
     def own_panel(k, carry):
         panel = col * own + k
@@ -286,17 +321,21 @@
         diagonal = jnp.sum(jnp.where(i_at == j_at, gram, 0.0), axis=0, keepdims=True)
         sums_send[k, size : size + 8, :] = jnp.broadcast_to(diagonal, (8, size))
 
-        @pl.when(owner_row(k) != row)
+        @pl.when(jnp.logical_not(collects))
         def _():
-            sums_copy(k).start()
-
-        @pl.when(owner_row(k) == row)
+            plane_copy(k, low_row).start()
+
+        @pl.when(jnp.logical_and(collects, k > 0))
         def _():
-            sums_slots[row] = sums_send[k]
+            collect(k - 1)
 
         return carry
 
     lax.fori_loop(0, own, own_panel, 0)
+
+    @pl.when(collects)
+    def _():
+        collect(own - 1)
 
     def form_rest(n, carry):
         form_group(lax.rem(col + n, cols))
@@ -305,41 +344,47 @@
     late = max(1, cols - 1)
     lax.fori_loop(1, late, form_rest, 0)
 
-    mine = row // spread
-    owns = owner_row(mine) == row
-
-    def update_copy(step):
-        other = lax.rem(me + step, total)
+    def relay_copy(step):
+        other = lax.rem(high_row + step, own)
+        return pltpu.make_async_remote_copy(
+            src_ref=relay.at[high_row],
+            dst_ref=relay.at[high_row],
+            send_sem=relay_send_sem.at[step],
+            recv_sem=relay_recv_sem.at[high_row],
+            device_id=(other * spread + low_row, col),
+            device_id_type=MESH,
+        )
+
+    def update_copy(k, step):
+        other = lax.rem(low_row * cols + col + step, spread * cols)
         other_col = lax.rem(other, cols)
         return pltpu.make_async_remote_copy(
-            src_ref=v_send.at[other_col],
-            dst_ref=update_out.at[col * own + mine],
-            send_sem=v_send_sem.at[step],
-            recv_sem=v_recv_sem.at[col * own + mine],
-            device_id=(other // cols, other_col),
+            src_ref=relay.at[k, other_col],
+            dst_ref=update_out.at[col * own + k],
+            send_sem=v_send_sem.at[k, step],
+            recv_sem=v_recv_sem.at[col * own + k],
+            device_id=(high_row * spread + other // cols, other_col),
             device_id_type=MESH,
         )
 
-    @pl.when(owns)
-    def _():
-        panel = col * own + mine
-
-        def arrive(step, carry):
-            other = lax.rem(row + step, rows)
-            pltpu.make_async_remote_copy(
-                src_ref=sums_send.at[0],
-                dst_ref=sums_slots.at[other],
-                send_sem=sums_send_sem.at[0],
-                recv_sem=sums_recv_sem.at[other],
-                device_id=(other, col),
-                device_id_type=MESH,
-            ).wait_recv()
+    def forward(k):
+        def send_update(step, carry):
+            update_copy(k, step).start()
             return carry
 
-        lax.fori_loop(1, rows, arrive, 0)
-        sums = lax.fori_loop(
-            1, rows, lambda r, a: a + sums_slots[r], sums_slots[0]
-        )
+        lax.fori_loop(1, spread * cols, send_update, 0)
+        update_out[col * own + k] = relay[k, col]
+
+    @pl.when(collects)
+    def _():
+        panel = col * own + high_row
+
+        def arrive(step, total_sums):
+            other = lax.rem(high_row + step, own)
+            sums_copy(high_row, other).wait_recv()
+            return total_sums + sums_slots[other]
+
+        sums = lax.fori_loop(1, own, arrive, sums_send[high_row])
         packed = sums[0:size, :]
         diagonal = sums[size : size + 1, :]
         turned = jnp.transpose(packed)
@@ -364,35 +409,51 @@
             jnp.sum(jnp.where(on_diagonal, projected, 0.0), axis=0, keepdims=True) / diagonal
         )
         for c in range(cols):
-            v_send[c, 0:width, :] = v_full[c * width : (c + 1) * width, :]
-            v_send[c, width : width + 8, :] = jnp.broadcast_to(new_roots, (8, size))
-
-        def send_update(step, carry):
-            update_copy(step).start()
+            lanes = slice(c * width, (c + 1) * width)
+            relay[high_row, c, 0:width, :] = v_full[lanes, :]
+            relay[high_row, c, width : width + 8, 0:width] = jnp.broadcast_to(
+                new_roots[:, lanes], (8, width)
+            )
+        for step in range(1, own):
+            relay_copy(step).start()
+        forward(high_row)
+
+    lax.fori_loop(late, cols, form_rest, 0)
+
+    @pl.when(collects)
+    def _():
+        def pass_on(step, carry):
+            k = lax.rem(high_row + step, own)
+            pltpu.make_async_remote_copy(
+                src_ref=relay.at[k],
+                dst_ref=relay.at[k],
+                send_sem=relay_send_sem.at[step],
+                recv_sem=relay_recv_sem.at[k],
+                device_id=(k * spread + low_row, col),
+                device_id_type=MESH,
+            ).wait_recv()
+            forward(k)
             return carry
 
-        lax.fori_loop(1, total, send_update, 0)
-        update_out[panel] = v_send[col]
-
-    lax.fori_loop(late, cols, form_rest, 0)
+        lax.fori_loop(1, own, pass_on, 0)
 
     def out_copy(n):
-        panel = lax.rem(n, cols) * own + n // cols
+        panel = lax.rem(n, cols) * own + lax.rem(high_row + n // cols, own)
         return pltpu.make_async_copy(
             stage.at[lax.rem(n, own)], refined_hbm.at[panel], out_sem.at[lax.rem(n, own)]
         )
 
     def finish(n, carry):
-        c, k = lax.rem(n, cols), n // cols
+        c, k = lax.rem(n, cols), lax.rem(high_row + n // cols, own)
         panel = c * own + k
-        from_row = k * spread + lax.rem(c, spread)
+        from_row = high_row * spread + lax.rem(c, spread)
 
         @pl.when(jnp.logical_or(row != from_row, col != c))
         def _():
             pltpu.make_async_remote_copy(
-                src_ref=v_send.at[0],
+                src_ref=relay.at[0, 0],
                 dst_ref=update_out.at[panel],
-                send_sem=v_send_sem.at[0],
+                send_sem=v_send_sem.at[0, 0],
                 recv_sem=v_recv_sem.at[panel],
                 device_id=(from_row, c),
                 device_id_type=MESH,
@@ -404,7 +465,7 @@
             formed[panel],
             preferred_element_type=jnp.float32,
         )
-        roots_out[panel] = update_out[panel, width : width + 8, :]
+        roots_out[pl.ds(panel, 1), :] = update_out[panel, width : width + 1, 0:width]
 
         @pl.when(n >= own)
         def _():
@@ -416,19 +477,25 @@
 
     lax.fori_loop(0, panels, finish, 0)
 
-    @pl.when(owns)
-    def _():
-        def sent(step, carry):
-            update_copy(step).wait_send()
+    @pl.when(collects)
+    def _():
+        def sent(n, carry):
+            update_copy(n // (spread * cols - 1), 1 + lax.rem(n, spread * cols - 1)).wait_send()
             return carry
 
-        lax.fori_loop(1, total, sent, 0)
-
-    for k in range(own):
-
-        @pl.when(owner_row(k) != row)
-        def _():
-            sums_copy(k).wait_send()
+        lax.fori_loop(0, own * (spread * cols - 1), sent, 0)
+        for step in range(1, own):
+            relay_copy(step).wait_send()
+        for k in range(own):
+
+            @pl.when(high_row != k)
+            def _():
+                sums_copy(k, high_row).wait_send()
+
+    @pl.when(jnp.logical_not(collects))
+    def _():
+        for k in range(own):
+            plane_copy(k, low_row).wait_send()
 
     @pl.when(row < rows - 1)
     def _():
@@ -460,7 +527,9 @@
     width = size // cols
     own = panels // cols
     total = rows * cols
-    own_pad = -(-own // 8) * 8
+    spread = rows // own
+    sub = size // LANES
+    squares_pad = -(-own * sub // 8) * 8
     vmem = pl.BlockSpec(memory_space=pltpu.VMEM)
     f32, bf16 = jnp.float32, jnp.bfloat16
     dma = pltpu.SemaphoreType.DMA
@@ -469,7 +538,7 @@
         functools.partial(merge_kernel, rows, cols),
         out_shape=(
             jax.ShapeDtypeStruct((panels, width, here), f32),
-            jax.ShapeDtypeStruct((panels, 8, size), f32),
+            jax.ShapeDtypeStruct((panels, width), f32),
         ),
         in_specs=[vmem] * 6 + [anywhere] * 3,
         out_specs=(anywhere, vmem),
@@ -483,16 +552,17 @@
             pltpu.VMEM((16, here), f32),
             pltpu.VMEM((16, block), f32),
             pltpu.VMEM((block, block), bf16),
-            pltpu.VMEM((own_pad, size), f32),
-            pltpu.VMEM((total, own_pad, size), f32),
+            pltpu.VMEM((squares_pad, LANES), f32),
+            pltpu.VMEM((total, squares_pad, LANES), f32),
             pltpu.VMEM((panels, size, LANES), f32),
             pltpu.VMEM((block_count, 2, block, block), bf16),
             pltpu.VMEM((panels, size, here), bf16),
             pltpu.VMEM((size, block), bf16),
             pltpu.VMEM((own, size + 8, size), f32),
-            pltpu.VMEM((rows, size + 8, size), f32),
+            pltpu.VMEM((own, spread, size + 8, size), f32),
+            pltpu.VMEM((own, size + 8, size), f32),
             pltpu.VMEM((size, size), f32),
-            pltpu.VMEM((cols, width + 8, size), f32),
+            pltpu.VMEM((own, cols, width + 8, size), f32),
             dma((3,)),
             dma((own,)),
             dma((2,)),
@@ -500,8 +570,12 @@
             dma((total,)),
             dma((total,)),
             dma((own,)),
-            dma((rows,)),
-            dma((total,)),
+            dma((own, spread)),
+            dma((own,)),
+            dma((own,)),
+            dma((own,)),
+            dma((own,)),
+            dma((own, spread * cols)),
             dma((panels,)),
         ],
         compiler_params=pltpu.CompilerParams(
@@ -518,9 +592,6 @@
         q_blocks,
         diag_blocks,
         coupling_blocks,
-    )
-    new_roots = lax.dynamic_slice_in_dim(
-        new_roots[:, 0, :], lax.axis_index("col") * width, width, 1
     )
     return (jnp.swapaxes(refined, 1, 2), new_roots)
 

time: 110 us -> 94.4 us (0.86)
  the two profiles are of different devices: /device:TPU:23 before, /device:TPU:21 now
where the time goes in v3:
time: 94.4 us; the launch traced here: 94.2 us
  Pallas kernels  85 us (90%)
  local copies, waits for them, and re-layouts  8.5 us (9%)
    pallas_call x1, Pallas kernels, shards(): pl.pallas_call(functools.partial(merge_kernel, rows, cols), out_shape=(ja...  85 us
    unnamed x4, local copies, waits for them, and re-layouts  8.5 us

profile of v3, /device:TPU:21, one launch (start us, length us, event | category | flops | bytes accessed | tf_op | source)
XLA Modules:
  0.0 94.2 jit_solution(11345470128732124071)
XLA Ops:
  0.6 85.0 %merge.1 = (f32[16,64,2048]{2,1,0:T(8,128)}, f32[16,64]{1,0:T(8,128)}) custom-call(f32[1,2048]{1,0:T(1,128)} %bitcast.6, f32[1,2048]{1,0:T(1,128)} %bitcast.7, s32[1,2048]{1,0:T(1,128)} %bitcast.8, f32[1,2048]{1,0:T(1,128)} %bitcast.9, f32[16,256]{1,0:T(8,128)} %roots_ref.1, s32[16,256]{1,0:T(8,128)} %order_ref.1, bf16[4,512,512]{2,1,0:T(8,128)(2,1)} %q_hbm.1, ...), custom_call_target="tpu_custom_call" | custom-call | tf_op jit(solution)/shard_map/merge/pallas_call | solution.py:537
  85.7 0.0 copy-start
  85.7 7.9 %copy.13 = f32[16,2048,64]{1,2,0:T(8,128)} copy(f32[16,2048,64]{1,2,0:T(8,128)} %bitcast.5) | data formatting | bytes 16777216
  93.6 0.0 copy-done
  93.6 0.6 copy.14
Async XLA Ops:
  85.7 7.9 %copy-start = (f32[16,64]{1,0:T(8,128)S(1)}, f32[16,64]{1,0:T(8,128)}, u32[]{:S(2)}) copy-start(f32[16,64]{1,0:T(8,128)} %get-tuple-element.9) | copy-start | bytes 12292

commit v4 on v3

--- a/solution.py
+++ b/solution.py
@@ -57,6 +57,7 @@
     sq_slots,
     factor_col,
     hmat,
+    onsite_col,
     formed,
     halo,
     sums_send,
@@ -205,6 +206,9 @@
     for b in range(block_count):
         hmat[b, 0] = coup_ref[b].astype(jnp.bfloat16)
         hmat[b, 1] = (0.5 * diag_ref[b]).astype(jnp.bfloat16)
+        onsite_col[b * block : (b + 1) * block, :] = column_form(
+            0.5 * onsite_ref[0:1, b * block : (b + 1) * block]
+        )
 
     def await_squares(step, carry):
         other = lax.rem(me + step, total)
@@ -221,7 +225,7 @@
 
     lax.fori_loop(1, total, await_squares, 0)
 
-    for c in range(cols):
+    def make_factors(c):
         sums = lax.fori_loop(
             0, rows, lambda r, a: a + sq_slots[r * cols + c], jnp.zeros(sq_send.shape, jnp.float32)
         )
@@ -233,32 +237,41 @@
                 )
             )
 
-    def form_block(poles, weight_row, panel, q_block):
-        scaled = cauchy_of(poles, weight_row, panel) * widen(factor_col[panel], block)
-        return dot_nt(scaled.astype(jnp.bfloat16), q_block).astype(jnp.bfloat16)
-
-    def form_panel(panel):
+    def form_block(poles, weight_row, group, q_block, store):
+        scaled = [
+            cauchy_of(poles, weight_row, group * own + k) * widen(factor_col[group * own + k], block)
+            for k in range(own)
+        ]
+        scaled = jnp.concatenate([part.astype(jnp.bfloat16) for part in scaled], axis=0)
+        result = dot_nt(scaled, q_block).astype(jnp.bfloat16)
+        for k in range(own):
+            store(k, result[k * size : (k + 1) * size])
+
+    def form_group(group):
+        make_factors(group)
         for b in range(block_count):
             lanes = pl.ds(b * block, block)
-            formed[panel, :, lanes] = form_block(pw[0:1, lanes], pw[8:9, lanes], panel, q_ref[b])
-
-    def form_group(group):
-        for b in range(block_count):
-            lanes = pl.ds(b * block, block)
-            scaled = [
-                cauchy_of(pw[0:1, lanes], pw[8:9, lanes], group * own + k)
-                * widen(factor_col[group * own + k], block)
-                for k in range(own)
-            ]
-            scaled = jnp.concatenate([part.astype(jnp.bfloat16) for part in scaled], axis=0)
-            result = dot_nt(scaled, q_ref[b]).astype(jnp.bfloat16)
-            for k in range(own):
-                formed[group * own + k, :, lanes] = result[k * size : (k + 1) * size]
+
+            def store(k, value):
+                formed[group * own + k, :, lanes] = value
+
+            form_block(pw[0:1, lanes], pw[8:9, lanes], group, q_ref[b], store)
+
+    form_group(col)
 
     @pl.when(row > 0)
     def _():
         for copy in halo_copies:
             copy.wait_recv()
+
+        def store(k, value):
+            halo[k] = value
+
+        form_block(halo_pw[0:1, :], halo_pw[8:9, :], col, halo_q[...], store)
+
+    @pl.when(row == 0)
+    def _():
+        halo[...] = jnp.zeros_like(halo)
 
     def plane_copy(k, source_low):
         return pltpu.make_async_remote_copy(
@@ -295,27 +308,22 @@
 
     def own_panel(k, carry):
         panel = col * own + k
-        form_panel(panel)
-
-        @pl.when(row > 0)
-        def _():
-            halo[...] = form_block(halo_pw[0:1, :], halo_pw[8:9, :], panel, halo_q[...])
-
-        @pl.when(row == 0)
-        def _():
-            halo[...] = jnp.zeros_like(halo)
-
         gram = jnp.zeros((size, size), jnp.float32)
         half = jnp.zeros((size, size), jnp.float32)
+        before = jnp.transpose(halo[k])
         for b in range(block_count):
             lanes = pl.ds(b * block, block)
             now = formed[panel, :, lanes]
-            before = halo[...] if b == 0 else formed[panel, :, pl.ds((b - 1) * block, block)]
-            image = dot_nt(before, hmat[b, 0]) + dot_nt(now, hmat[b, 1])
-            image = image + 0.5 * onsite_ref[0:1, lanes] * now.astype(jnp.float32)
+            now_turned = jnp.transpose(now)
+            image = jnp.dot(hmat[b, 0], before, preferred_element_type=jnp.float32)
+            image = image + jnp.dot(hmat[b, 1], now_turned, preferred_element_type=jnp.float32)
+            onsite = widen(onsite_col[b * block : (b + 1) * block, :], size)
+            image = image + onsite * now_turned.astype(jnp.float32)
             high, low = split(image)
-            gram = gram + dot_nt(now, now)
-            half = half + dot_nt(now, high) + dot_nt(now, low)
+            gram = gram + jnp.dot(now, now_turned, preferred_element_type=jnp.float32)
+            half = half + jnp.dot(now, high, preferred_element_type=jnp.float32)
+            half = half + jnp.dot(now, low, preferred_element_type=jnp.float32)
+            before = now_turned
         projected = half + jnp.transpose(half)
         sums_send[k, 0:size, :] = jnp.where(j_at > i_at, gram, projected)
         diagonal = jnp.sum(jnp.where(i_at == j_at, gram, 0.0), axis=0, keepdims=True)
@@ -556,8 +564,9 @@
             pltpu.VMEM((total, squares_pad, LANES), f32),
             pltpu.VMEM((panels, size, LANES), f32),
             pltpu.VMEM((block_count, 2, block, block), bf16),
+            pltpu.VMEM((here, LANES), f32),
             pltpu.VMEM((panels, size, here), bf16),
-            pltpu.VMEM((size, block), bf16),
+            pltpu.VMEM((own, size, block), bf16),
             pltpu.VMEM((own, size + 8, size), f32),
             pltpu.VMEM((own, spread, size + 8, size), f32),
             pltpu.VMEM((own, size + 8, size), f32),

time: 94.4 us -> 91.7 us (0.971)
  Pallas kernels: 85 us -> 82.3 us
    pallas_call x1, Pallas kernels: 85 us -> 82.3 us  [shards(): pl.pallas_call(functools.partial(merge_kernel, rows, cols), out_shape=(ja...]
where the time goes in v4:
time: 91.7 us; the launch traced here: 91.5 us
  Pallas kernels  82.3 us (90%)
  local copies, waits for them, and re-layouts  8.5 us (9%)
    pallas_call x1, Pallas kernels, shards(): pl.pallas_call(functools.partial(merge_kernel, rows, cols), out_shape=(ja...  82.3 us
    unnamed x4, local copies, waits for them, and re-layouts  8.5 us

profile of v4, /device:TPU:21, one launch (start us, length us, event | category | flops | bytes accessed | tf_op | source)
XLA Modules:
  0.0 91.5 jit_solution(7218561378390308398)
XLA Ops:
  0.6 82.3 %merge.1 = (f32[16,64,2048]{2,1,0:T(8,128)}, f32[16,64]{1,0:T(8,128)}) custom-call(f32[1,2048]{1,0:T(1,128)} %bitcast.6, f32[1,2048]{1,0:T(1,128)} %bitcast.7, s32[1,2048]{1,0:T(1,128)} %bitcast.8, f32[1,2048]{1,0:T(1,128)} %bitcast.9, f32[16,256]{1,0:T(8,128)} %roots_ref.1, s32[16,256]{1,0:T(8,128)} %order_ref.1, bf16[4,512,512]{2,1,0:T(8,128)(2,1)} %q_hbm.1, ...), custom_call_target="tpu_custom_call" | custom-call | tf_op jit(solution)/shard_map/merge/pallas_call | solution.py:545
  83.0 0.0 copy-start
  83.0 7.9 %copy.13 = f32[16,2048,64]{1,2,0:T(8,128)} copy(f32[16,2048,64]{1,2,0:T(8,128)} %bitcast.5) | data formatting | bytes 16777216
  90.9 0.0 copy-done
  90.9 0.6 copy.14
Async XLA Ops:
  83.0 7.9 %copy-start = (f32[16,64]{1,0:T(8,128)S(1)}, f32[16,64]{1,0:T(8,128)}, u32[]{:S(2)}) copy-start(f32[16,64]{1,0:T(8,128)} %get-tuple-element.9) | copy-start | bytes 12292

commit v5 on v4

--- a/solution.py
+++ b/solution.py
@@ -306,7 +306,8 @@
         def _():
             sums_copy(k, high_row).start()
 
-    def own_panel(k, carry):
+    def own_panel(step, carry):
+        k = lax.rem(high_row + 1 + step, own)
         panel = col * own + k
         gram = jnp.zeros((size, size), jnp.float32)
         half = jnp.zeros((size, size), jnp.float32)
@@ -333,23 +334,19 @@
         def _():
             plane_copy(k, low_row).start()
 
-        @pl.when(jnp.logical_and(collects, k > 0))
+        @pl.when(jnp.logical_and(collects, step > 0))
         def _():
-            collect(k - 1)
+            collect(lax.rem(high_row + step, own))
 
         return carry
 
     lax.fori_loop(0, own, own_panel, 0)
-
-    @pl.when(collects)
-    def _():
-        collect(own - 1)
 
     def form_rest(n, carry):
         form_group(lax.rem(col + n, cols))
         return carry
 
-    late = max(1, cols - 1)
+    late = min(2, cols)
     lax.fori_loop(1, late, form_rest, 0)
 
     def relay_copy(step):
@@ -386,6 +383,7 @@
     @pl.when(collects)
     def _():
         panel = col * own + high_row
+        collect(high_row)
 
         def arrive(step, total_sums):
             other = lax.rem(high_row + step, own)
@@ -426,24 +424,33 @@
             relay_copy(step).start()
         forward(high_row)
 
-    lax.fori_loop(late, cols, form_rest, 0)
+    def pass_on(step, carry):
+        k = lax.rem(high_row + step, own)
+        pltpu.make_async_remote_copy(
+            src_ref=relay.at[k],
+            dst_ref=relay.at[k],
+            send_sem=relay_send_sem.at[step],
+            recv_sem=relay_recv_sem.at[k],
+            device_id=(k * spread + low_row, col),
+            device_id_type=MESH,
+        ).wait_recv()
+        forward(k)
+        return carry
+
+    def form_and_pass(n, carry):
+        form_rest(n, carry)
+
+        @pl.when(jnp.logical_and(collects, n - late + 1 < own))
+        def _():
+            pass_on(n - late + 1, 0)
+
+        return carry
+
+    lax.fori_loop(late, cols, form_and_pass, 0)
 
     @pl.when(collects)
     def _():
-        def pass_on(step, carry):
-            k = lax.rem(high_row + step, own)
-            pltpu.make_async_remote_copy(
-                src_ref=relay.at[k],
-                dst_ref=relay.at[k],
-                send_sem=relay_send_sem.at[step],
-                recv_sem=relay_recv_sem.at[k],
-                device_id=(k * spread + low_row, col),
-                device_id_type=MESH,
-            ).wait_recv()
-            forward(k)
-            return carry
-
-        lax.fori_loop(1, own, pass_on, 0)
+        lax.fori_loop(min(own, 1 + cols - late), own, pass_on, 0)
 
     def out_copy(n):
         panel = lax.rem(n, cols) * own + lax.rem(high_row + n // cols, own)

time: 91.7 us -> 83.4 us (0.909)
  the two profiles are of different devices: /device:TPU:21 before, /device:TPU:23 now
where the time goes in v5:
time: 83.4 us; the launch traced here: 82.3 us
  Pallas kernels  73.2 us (88%)
  local copies, waits for them, and re-layouts  8.5 us (10%)
    pallas_call x1, Pallas kernels, shards(): pl.pallas_call(functools.partial(merge_kernel, rows, cols), out_shape=(ja...  73.2 us
    unnamed x4, local copies, waits for them, and re-layouts  8.5 us

profile of v5, /device:TPU:23, one launch (start us, length us, event | category | flops | bytes accessed | tf_op | source)
XLA Modules:
  0.0 82.3 jit_solution(5395430790367300709)
XLA Ops:
  0.6 73.2 %merge.1 = (f32[16,64,2048]{2,1,0:T(8,128)}, f32[16,64]{1,0:T(8,128)}) custom-call(f32[1,2048]{1,0:T(1,128)} %bitcast.6, f32[1,2048]{1,0:T(1,128)} %bitcast.7, s32[1,2048]{1,0:T(1,128)} %bitcast.8, f32[1,2048]{1,0:T(1,128)} %bitcast.9, f32[16,256]{1,0:T(8,128)} %roots_ref.1, s32[16,256]{1,0:T(8,128)} %order_ref.1, bf16[4,512,512]{2,1,0:T(8,128)(2,1)} %q_hbm.1, ...), custom_call_target="tpu_custom_call" | custom-call | tf_op jit(solution)/shard_map/merge/pallas_call | solution.py:552
  73.8 0.0 copy-start
  73.8 7.9 %copy.13 = f32[16,2048,64]{1,2,0:T(8,128)} copy(f32[16,2048,64]{1,2,0:T(8,128)} %bitcast.5) | data formatting | bytes 16777216
  81.7 0.0 copy-done
  81.7 0.6 copy.14
Async XLA Ops:
  73.8 7.9 %copy-start = (f32[16,64]{1,0:T(8,128)S(1)}, f32[16,64]{1,0:T(8,128)}, u32[]{:S(2)}) copy-start(f32[16,64]{1,0:T(8,128)} %get-tuple-element.9) | copy-start | bytes 12292
